TPU v7x, 128 devices: a whole 4x4x4 slice. The times are simulated.
128 devices in a mesh: row: 8 (over y_lo, x), col: 16 (over z, y_hi, core).
Axes of the slice: x: 4, y: 4 (y_hi: 2, y_lo: 2; y = y_hi * 2 + y_lo), z: 4, core: 2. Of those that a mesh axis runs over, the one named last changes fastest.
Arguments:
- tokens: bfloat16 [2048, 28672], P('row', 'col'), may hold values from -6 to 6
- edit_src: int32 [512, 4], replicated, may hold values from 0 to 2047
- cov_tiles: float32 [8, 16, 1792, 1792], P('row', 'col'), as said below
- cov_far: float32 [16, 896, 1792], P('col', 'row'), may hold values from -0.03125 to 0.03125
- residual: bfloat16 [8192, 512], P('row'), may hold values from -0.25 to 0.25
Outputs:
- delta: bfloat16 [8192, 28672], P('row', 'col')
Inputs may be any that keep to these rules, and one draw needn't show every extreme that they name: cov_tiles[0, b] is symmetric for every b.
All inputs are finite; a program needn't handle non-finite values.
Results may differ from a plain program's by a relative error of at most 0.024.
Values may be sent and summed in bfloat16 or wider, within the bound.
A program may use at most 128 MiB of HBM per device.

v0:
```python
import jax
import jax.numpy as jnp
from jax import lax
from jax.sharding import PartitionSpec as P


def passed_along(value, axis, steps):
    count = lax.axis_size(axis)
    pairs = [(source, (source + steps) % count) for source in range(count)]
    return lax.ppermute(value, axis, pairs)


def from_partner(value, axis, apart):
    mask = 2**apart
    pairs = [(source, source ^ mask) for source in range(lax.axis_size(axis))]
    return lax.ppermute(value, axis, pairs)


def shards(tokens, edit_src, cov_tiles, cov_far, residual):
    highest = lax.Precision.HIGHEST
    rows_axis = lax.axis_size("row")
    row_at = lax.axis_index("row")
    col_at = lax.axis_index("col")
    tok_dev = tokens.shape[0]
    tile_width = tokens.shape[1]
    relative = edit_src - row_at * tok_dev
    slot_ids = lax.broadcasted_iota(jnp.int32, (1, 1, tok_dev), 2)
    counts = (
        jnp.sum((relative[:, :, None] == slot_ids).astype(jnp.float32), axis=1) / edit_src.shape[1]
    )
    partial_keys = jnp.dot(counts.astype(jnp.bfloat16), tokens, preferred_element_type=jnp.float32)
    own_keys = lax.psum(partial_keys.astype(jnp.bfloat16), "row")
    bit_count = rows_axis.bit_length() - 1
    lagged = own_keys
    for bit_level in range(bit_count):
        shifted = passed_along(lagged, "col", 2**bit_level)
        lagged = jnp.where((row_at >> bit_level) % 2 == 1, shifted, lagged)
    cov_block = cov_tiles[0, 0]
    own_float = own_keys.astype(jnp.float32)
    direct = jnp.dot(
        lagged.astype(jnp.float32), cov_block, precision=highest, preferred_element_type=jnp.float32
    )
    mirror = lax.cond(
        row_at > 0,
        lambda: jnp.dot(
            own_float, cov_block.T, precision=highest, preferred_element_type=jnp.float32
        ),
        lambda: jnp.zeros_like(direct),
    )
    for bit_level in range(bit_count):
        shifted = passed_along(mirror.astype(jnp.bfloat16), "col", -(2**bit_level)).astype(
            mirror.dtype
        )
        mirror = jnp.where((row_at >> bit_level) % 2 == 1, shifted, mirror)
    far_slab = cov_far[0]
    far_rows = far_slab.shape[0]
    low_half = col_at < rows_axis
    half_index = col_at // rows_axis
    offset = half_index * (tile_width // 2) + row_at * far_rows
    other_keys = from_partner(own_keys, "col", bit_count)
    keys_low = jnp.where(low_half, own_keys, other_keys).astype(jnp.float32)
    keys_high = jnp.where(low_half, other_keys, own_keys).astype(jnp.float32)
    picked = lax.dynamic_slice_in_dim(keys_low, offset, far_rows, 1)
    high_term = jnp.dot(picked, far_slab, precision=highest, preferred_element_type=jnp.float32)
    narrow = jnp.dot(keys_high, far_slab.T, precision=highest, preferred_element_type=jnp.float32)
    low_term = lax.dynamic_update_slice_in_dim(jnp.zeros_like(direct), narrow, offset, 1)
    kept_term = jnp.where(low_half, low_term, high_term)
    sent_term = jnp.where(low_half, high_term, low_term)
    far_total = kept_term + from_partner(sent_term.astype(jnp.bfloat16), "col", bit_count).astype(
        sent_term.dtype
    )
    summed = direct + mirror + far_total
    q_block = lax.psum(summed.astype(jnp.bfloat16), "row")
    return jnp.dot(residual, q_block, preferred_element_type=jnp.float32).astype(jnp.bfloat16)


def solution(mesh):
    placed = (
        P("row", "col"),
        P(),
        P("row", "col", None, None),
        P("col", "row", None),
        P("row", None),
    )
    return jax.shard_map(
        shards, mesh=mesh, in_specs=placed, out_specs=P("row", "col"), check_vma=False
    )
```

profile of v0, /device:TPU:0, one launch (start us, length us, event | category | flops | bytes accessed | tf_op | source)
XLA Modules:
  0.0 415.6 jit_solution(1574876981922074789)
XLA Ops:
  6.5 0.0 copy-start
  6.5 0.0 all-reduce.3.cloned.1.call-start
  6.5 0.8 broadcast_subtract_fusion
  7.3 0.3 convert_reduce_fusion
  7.7 3.1 convolution_convert_fusion.1
  10.7 0.0 all-reduce.3.cloned.1.call-update
  10.8 0.0 all-reduce.5.cloned.1.call-start
  10.8 83.3 %all-reduce.3.cloned.1.call-done = bf16[512,1792]{1,0:T(8,128)(2,1)} async-done(((bf16[512,1792]{1,0:T(8,128)(2,1)}), bf16[512,1792]{1,0:T(8,128)(2,1)}) %all-reduce.3.cloned.1.call-update) | async-done | bytes 1835024 | tf_op jit(solution)/shard_map/psum | solution.py:32
  94.1 0.0 collective-permute-start
  94.1 2.1 conditional.1
  94.1 2.1 broadcast.10
  96.2 3.4 convert_element_type.56
  99.7 5.4 %collective-permute-start.3 = (bf16[512,1792]{1,0:T(8,128)(2,1)}, bf16[512,1792]{1,0:T(8,128)(2,1)S(1)}, u32[]{:S(2)}, u32[]{:S(2)}) collective-permute-start(bf16[512,1792]{1,0:T(8,128)(2,1)} %convert_element_type.56), channel_id=1, source_target_pairs={{0,15},{1,0},{2,1},{3,2},{4,3},{5,4},{6,5},{7,6},{8,7},{9,8},{10,9... | collective-permute-start | bytes 5505032 | tf_op jit(solution)/shard_map/ppermute | solution.py:10
  105.0 0.0 copy-start.1
  105.0 1.9 collective-permute-start.6
  107.0 24.4 %collective-permute-done = bf16[512,1792]{1,0:T(8,128)(2,1)} collective-permute-done((bf16[512,1792]{1,0:T(8,128)(2,1)}, bf16[512,1792]{1,0:T(8,128)(2,1)}, u32[]{:S(2)}, u32[]{:S(2)}) %collective-permute-start) | collective-permute-done | bytes 1835040 | tf_op jit(solution)/shard_map/ppermute | solution.py:10
  131.4 3.0 broadcast_select_fusion
  134.4 0.7 collective-permute-start.1
  135.1 6.4 %collective-permute-done.3 = bf16[512,1792]{1,0:T(8,128)(2,1)S(1)} collective-permute-done((bf16[512,1792]{1,0:T(8,128)(2,1)}, bf16[512,1792]{1,0:T(8,128)(2,1)S(1)}, u32[]{:S(2)}, u32[]{:S(2)}) %collective-permute-start.3) | collective-permute-done | bytes 1835040 | tf_op jit(solution)/shard_map/ppermute | solution.py:10
  141.4 0.0 copy-done.1
  141.4 0.0 copy-start.5
  141.4 1.9 fusion.1
  143.4 1.0 collective-permute-start.4
  144.4 56.9 %collective-permute-done.6 = bf16[512,1792]{1,0:T(8,128)(2,1)} collective-permute-done((bf16[512,1792]{1,0:T(8,128)(2,1)}, bf16[512,1792]{1,0:T(8,128)(2,1)}, u32[]{:S(2)}, u32[]{:S(2)}) %collective-permute-start.6) | collective-permute-done | bytes 1835040 | tf_op jit(solution)/shard_map/ppermute | solution.py:16
  201.3 3.3 fusion.2
  204.6 2.1 broadcast.12
  206.7 1.8 dynamic_update_slice.3
  208.5 0.0 copy-start.4
  208.5 0.0 copy-start.6
  208.5 0.0 collective-permute-done.1
  208.5 3.1 broadcast_select_fusion.1
  211.6 0.0 collective-permute-start.2
  211.6 0.0 copy-done.4
  211.7 0.0 copy-done.6
  211.7 0.0 copy-start.2
  211.7 5.4 %select_convert_fusion = (bf16[512,1792]{1,0:T(8,128)(2,1)}, f32[512,1792]{1,0:T(8,128)}) fusion(f32[512,1792]{1,0:T(8,128)S(1)} %copy-done.4, pred[]{:T(512)S(6)} %lt.30, f32[1,112,1792]{2,1,0:T(8,128)S(1)} %copy-done.6, bf16[512,1792]{1,0:T(8,128)(2,1)} %collective-permute-done.6, s32[]{:T(128)S(6)} %select_n.96, ...), kind=kOutput, calls=%fused_computation.2 | convolution fusion | flops 1234100224 | bytes 10241536 | tf_op jit(solution)/shard_map/dot_general | solution.py:64
  217.1 0.0 collective-permute-start.7
  217.1 0.8 collective-permute-done.4
  217.9 0.0 copy-done.5
  217.9 0.0 copy-done.2
  217.9 3.5 fusion.8
  221.4 2.4 collective-permute-start.5
  223.8 70.5 %collective-permute-done.2 = bf16[512,1792]{1,0:T(8,128)(2,1)} collective-permute-done((bf16[512,1792]{1,0:T(8,128)(2,1)}, bf16[512,1792]{1,0:T(8,128)(2,1)}, u32[]{:S(2)}, u32[]{:S(2)}) %collective-permute-start.2) | collective-permute-done | bytes 1835040 | tf_op jit(solution)/shard_map/ppermute | solution.py:10
  294.3 0.0 copy-start.3
  294.3 19.6 %fusion.4 = f32[512,1792]{1,0:T(8,128)} fusion(bf16[512,1792]{1,0:T(8,128)(2,1)} %collective-permute-done.2, bf16[512,1792]{1,0:T(8,128)(2,1)} %broadcast_select_fusion.1, pred[]{:T(512)S(6)} %eq.32, f32[1,1,1792,1792]{3,2,1,0:T(8,128)} %param.9), kind=kOutput, calls=%fused_computation.12 | convolution fusion | flops 19730923520 | bytes 20185088 | tf_op jit(solution)/shard_map/dot_general | solution.py:40
  313.9 0.0 collective-permute-done.7
  313.9 0.0 collective-permute-done.5
  313.9 0.0 copy-done.3
  313.9 8.1 %add_convert_fusion = bf16[512,1792]{1,0:T(8,128)(2,1)} fusion(bf16[512,1792]{1,0:T(8,128)(2,1)} %collective-permute-done.7, f32[512,1792]{1,0:T(8,128)} %dynamic_update_slice.3, f32[512,1792]{1,0:T(8,128)} %get-tuple-element.16, f32[512,1792]{1,0:T(8,128)} %fusion.4, bf16[512,1792]{1,0:T(8,128)(2,1)} %collective-permute-done.5, pred[]{:T(512)S(6)} %lt.30, ...), kind=kLoop, calls=%fused_computation.1 | loop fusion | flops 11010048 | bytes 23855108 | tf_op jit(solution)/shard_map/convert_element_type | solution.py:73
  322.0 0.0 all-reduce.5.cloned.1.call-update
  322.0 75.4 %all-reduce.5.cloned.1.call-done = bf16[512,1792]{1,0:T(8,128)(2,1)} async-done(((bf16[512,1792]{1,0:T(8,128)(2,1)}), bf16[512,1792]{1,0:T(8,128)(2,1)}) %all-reduce.5.cloned.1.call-update) | async-done | bytes 1835024 | tf_op jit(solution)/shard_map/psum | solution.py:73
  397.4 0.0 copy-done
  397.4 5.4 %fusion = bf16[1024,1792]{0,1:T(8,128)(2,1)} fusion(bf16[512,1792]{1,0:T(8,128)(2,1)} %all-reduce.5.cloned.1.call-done, bf16[1024,512]{1,0:T(8,128)(2,1)S(1)} %copy-done), kind=kOutput, calls=%fused_computation.5 | convolution fusion | flops 1880883200 | bytes 6553600 | tf_op jit(solution)/shard_map/dot_general | solution.py:74
  402.8 5.9 %copy.10 = bf16[1024,1792]{1,0:T(8,128)(2,1)} copy(bf16[1024,1792]{0,1:T(8,128)(2,1)} %fusion) | data formatting | bytes 7340032 | tf_op jit(solution)/shard_map/convert_element_type | solution.py:74
Async XLA Ops:
  6.5 390.9 %copy-start = (bf16[1024,512]{1,0:T(8,128)(2,1)S(1)}, bf16[1024,512]{1,0:T(8,128)(2,1)}, u32[]{:S(2)}) copy-start(bf16[1024,512]{1,0:T(8,128)(2,1)} %param.11) | copy-start | bytes 3145732
  6.5 87.6 %all-reduce.3.cloned.1.call-start = ((), (), s32[]{:S(2)}) async-start(), calls=%async_computation | async-start | bytes 3670016 | tf_op jit(solution)/shard_map/psum | solution.py:32
  10.8 386.6 %all-reduce.5.cloned.1.call-start = ((), (), s32[]{:S(2)}) async-start(), calls=%async_computation.1 | async-start | bytes 3670016 | tf_op jit(solution)/shard_map/psum | solution.py:73
  94.1 37.3 %collective-permute-start = (bf16[512,1792]{1,0:T(8,128)(2,1)}, bf16[512,1792]{1,0:T(8,128)(2,1)}, u32[]{:S(2)}, u32[]{:S(2)}) collective-permute-start(bf16[512,1792]{1,0:T(8,128)(2,1)} %all-reduce.3.cloned.1.call-done), channel_id=1, source_target_pairs={{0,1},{1,2},{2,3},{3,4},{4,5},{5,6},{6,7},{7,8},{8,9},{9,10},{10,1... | collective-permute-start | bytes 5505032 | tf_op jit(solution)/shard_map/ppermute | solution.py:10
  99.7 41.7 %collective-permute-start.3 = (bf16[512,1792]{1,0:T(8,128)(2,1)}, bf16[512,1792]{1,0:T(8,128)(2,1)S(1)}, u32[]{:S(2)}, u32[]{:S(2)}) collective-permute-start(bf16[512,1792]{1,0:T(8,128)(2,1)} %convert_element_type.56), channel_id=1, source_target_pairs={{0,15},{1,0},{2,1},{3,2},{4,3},{5,4},{6,5},{7,6},{8,7},{9,8},{10,9... | collective-permute-start | bytes 5505032 | tf_op jit(solution)/shard_map/ppermute | solution.py:10
  105.0 36.4 %copy-start.1 = (f32[512,1792]{1,0:T(8,128)S(1)}, f32[512,1792]{1,0:T(8,128)}, u32[]{:S(2)}) copy-start(f32[512,1792]{1,0:T(8,128)} %get-tuple-element.17) | copy-start | bytes 11010052
  105.0 96.3 %collective-permute-start.6 = (bf16[512,1792]{1,0:T(8,128)(2,1)}, bf16[512,1792]{1,0:T(8,128)(2,1)}, u32[]{:S(2)}, u32[]{:S(2)}) collective-permute-start(bf16[512,1792]{1,0:T(8,128)(2,1)} %all-reduce.3.cloned.1.call-done), channel_id=1, source_target_pairs={{0,8},{1,9},{2,10},{3,11},{4,12},{5,13},{6,14},{7,15},{8,0},{9,1},... | collective-permute-start | bytes 5505032 | tf_op jit(solution)/shard_map/ppermute | solution.py:16
  134.4 74.1 %collective-permute-start.1 = (bf16[512,1792]{1,0:T(8,128)(2,1)}, bf16[512,1792]{1,0:T(8,128)(2,1)}, u32[]{:S(2)}, u32[]{:S(2)}) collective-permute-start(bf16[512,1792]{1,0:T(8,128)(2,1)} %broadcast_select_fusion), channel_id=1, source_target_pairs={{0,2},{1,3},{2,4},{3,5},{4,6},{5,7},{6,8},{7,9},{8,10},{9,11},{10,... | collective-permute-start | bytes 5505032 | tf_op jit(solution)/shard_map/ppermute | solution.py:10
  141.4 76.5 %copy-start.5 = (bf16[512,1792]{1,0:T(8,128)(2,1)}, bf16[512,1792]{1,0:T(8,128)(2,1)S(1)}, u32[]{:S(2)}) copy-start(bf16[512,1792]{1,0:T(8,128)(2,1)S(1)} %collective-permute-done.3) | copy-start | bytes 5505028
  143.4 74.5 %collective-permute-start.4 = (bf16[512,1792]{1,0:T(8,128)(2,1)}, bf16[512,1792]{1,0:T(8,128)(2,1)}, u32[]{:S(2)}, u32[]{:S(2)}) collective-permute-start(bf16[512,1792]{1,0:T(8,128)(2,1)} %fusion.1), channel_id=1, source_target_pairs={{0,14},{1,15},{2,0},{3,1},{4,2},{5,3},{6,4},{7,5},{8,6},{9,7},{10,... | collective-permute-start | bytes 5505032 | tf_op jit(solution)/shard_map/ppermute | solution.py:10
  208.5 3.2 copy-start.4
  208.5 3.2 copy-start.6
  211.6 82.7 %collective-permute-start.2 = (bf16[512,1792]{1,0:T(8,128)(2,1)}, bf16[512,1792]{1,0:T(8,128)(2,1)}, u32[]{:S(2)}, u32[]{:S(2)}) collective-permute-start(bf16[512,1792]{1,0:T(8,128)(2,1)} %broadcast_select_fusion.1), channel_id=1, source_target_pairs={{0,4},{1,5},{2,6},{3,7},{4,8},{5,9},{6,10},{7,11},{8,12},{9,13},{1... | collective-permute-start | bytes 5505032 | tf_op jit(solution)/shard_map/ppermute | solution.py:10
  211.7 6.3 %copy-start.2 = (f32[512,1792]{1,0:T(8,128)S(1)}, f32[512,1792]{1,0:T(8,128)}, u32[]{:S(2)}) copy-start(f32[512,1792]{1,0:T(8,128)} %get-tuple-element.17) | copy-start | bytes 11010052
  217.1 96.8 %collective-permute-start.7 = (bf16[512,1792]{1,0:T(8,128)(2,1)}, bf16[512,1792]{1,0:T(8,128)(2,1)}, u32[]{:S(2)}, u32[]{:S(2)}) collective-permute-start(bf16[512,1792]{1,0:T(8,128)(2,1)} %get-tuple-element.15), channel_id=1, source_target_pairs={{0,8},{1,9},{2,10},{3,11},{4,12},{5,13},{6,14},{7,15},{8,0},{9,1},... | collective-permute-start | bytes 5505032 | tf_op jit(solution)/shard_map/ppermute | solution.py:16
  221.4 92.5 %collective-permute-start.5 = (bf16[512,1792]{1,0:T(8,128)(2,1)}, bf16[512,1792]{1,0:T(8,128)(2,1)}, u32[]{:S(2)}, u32[]{:S(2)}) collective-permute-start(bf16[512,1792]{1,0:T(8,128)(2,1)} %fusion.8), channel_id=1, source_target_pairs={{0,12},{1,13},{2,14},{3,15},{4,0},{5,1},{6,2},{7,3},{8,4},{9,5},{1... | collective-permute-start | bytes 5505032 | tf_op jit(solution)/shard_map/ppermute | solution.py:10
  294.3 19.6 %copy-start.3 = (f32[512,1792]{1,0:T(8,128)S(1)}, f32[512,1792]{1,0:T(8,128)}, u32[]{:S(2)}) copy-start(f32[512,1792]{1,0:T(8,128)} %get-tuple-element.17) | copy-start | bytes 11010052
Sparse Core Ops, SparseCore 0:
  10.9 83.1 all-reduce.2
  322.1 75.2 all-reduce.4
where the time goes:
time: 416 us
  waiting for transfers between devices  318 us (76%)
  matrix products  36.8 us (9%)
  other arithmetic  24.2 us (6%)
  between operations  13.5 us (3%)
  local copies, waits for them, and re-layouts  11.9 us (3%)
  starting transfers between devices  11.5 us (3%)
    ppermute x6, waiting for transfers between devices, passed_along(): return lax.ppermute(value, axis, pairs)  102 us
    psum x1, waiting for transfers between devices, shards(): own_keys = lax.psum(partial_keys.astype(jnp.bfloat16), 'row')  83.3 us
    psum x1, waiting for transfers between devices, shards(): q_block = lax.psum(summed.astype(jnp.bfloat16), 'row')  75.4 us
    ppermute x2, waiting for transfers between devices, from_partner(): return lax.ppermute(value, axis, pairs)  56.9 us
    dot_general x1, matrix products, shards(): jnp.dot(lagged.astype(jnp.float32), cov_block, precision=highest, preferr...  19.6 us
    ppermute x6, starting transfers between devices, passed_along(): return lax.ppermute(value, axis, pairs)  9.48 us
    convert_element_type x3, other arithmetic, shards(): mirror.astype(jnp.bfloat16)  8.85 us
  transfers between devices with their start and end apart: 10, of which 7 were waited for; matrix products, arithmetic and copies ran while one was open for 12% of the time, Pallas kernels for 0%

commit v1 on v0

--- a/solution.py
+++ b/solution.py
@@ -70,7 +70,7 @@
         sent_term.dtype
     )
     summed = direct + mirror + far_total
-    q_block = lax.psum(summed.astype(jnp.bfloat16), "row")
+    q_block = jnp.sum(lax.all_gather(summed.astype(jnp.bfloat16), "row"), axis=0)
     return jnp.dot(residual, q_block, preferred_element_type=jnp.float32).astype(jnp.bfloat16)
 
 

time: 416 us -> 494 us (1.19)
  waiting for transfers between devices: 318 us -> 388 us
  other arithmetic: 24.2 us -> 32.5 us
    all_gather x0 -> x1, waiting for transfers between devices: none -> 145 us  [shards(): lax.all_gather(summed.astype(jnp.bfloat16), 'row')]
    psum x1 -> x0, waiting for transfers between devices: 75.4 us -> none  [shards(): q_block = lax.psum(summed.astype(jnp.bfloat16), 'row')]
    reduce_sum x0 -> x1, other arithmetic: none -> 8.35 us  [shards(): jnp.sum(lax.all_gather(summed.astype(jnp.bfloat16), 'row'), axis=0)]
  transfers between devices with their start and end apart: 10 -> 10, of which waited for: 7 -> 7; matrix products, arithmetic and copies ran while one was open for 12% -> 10% of each run, Pallas kernels for 0% -> 0%
where the time goes in v1:
time: 494 us; the launch traced here: 492 us
  waiting for transfers between devices  388 us (79%)
  matrix products  35.3 us (7%)
  other arithmetic  32.5 us (7%)
  between operations  13.5 us (3%)
  local copies, waits for them, and re-layouts  11.9 us (2%)
  starting transfers between devices  11.5 us (2%)
    all_gather x1, waiting for transfers between devices, shards(): lax.all_gather(summed.astype(jnp.bfloat16), 'row')  145 us
    ppermute x6, waiting for transfers between devices, passed_along(): return lax.ppermute(value, axis, pairs)  102 us
    psum x1, waiting for transfers between devices, shards(): own_keys = lax.psum(partial_keys.astype(jnp.bfloat16), 'row')  83.3 us
    ppermute x2, waiting for transfers between devices, from_partner(): return lax.ppermute(value, axis, pairs)  56.9 us
    dot_general x1, matrix products, shards(): jnp.dot(lagged.astype(jnp.float32), cov_block, precision=highest, preferr...  19.6 us
  transfers between devices with their start and end apart: 10, of which 7 were waited for; matrix products, arithmetic and copies ran while one was open for 10% of the time, Pallas kernels for 0%

profile of v1, /device:TPU:0, one launch (start us, length us, event | category | flops | bytes accessed | tf_op | source)
XLA Modules:
  0.0 492.5 jit_solution(11601712822969154436)
XLA Ops:
  6.5 0.0 copy-start
  6.5 0.0 all-reduce.2.cloned.1.call-start
  6.5 0.8 broadcast_subtract_fusion
  7.3 0.3 convert_reduce_fusion
  7.7 3.1 convolution_convert_fusion.1
  10.7 0.0 all-reduce.2.cloned.1.call-update
  10.8 0.0 all-gather.3.cloned.1.call-start
  10.8 83.3 %all-reduce.2.cloned.1.call-done = bf16[512,1792]{1,0:T(8,128)(2,1)} async-done(((bf16[512,1792]{1,0:T(8,128)(2,1)}), bf16[512,1792]{1,0:T(8,128)(2,1)}) %all-reduce.2.cloned.1.call-update) | async-done | bytes 1835024 | tf_op jit(solution)/shard_map/psum | solution.py:32
  94.1 0.0 collective-permute-start
  94.1 2.1 conditional.1
  94.1 2.1 broadcast.10
  96.2 3.4 convert_element_type.58
  99.7 5.4 %collective-permute-start.3 = (bf16[512,1792]{1,0:T(8,128)(2,1)}, bf16[512,1792]{1,0:T(8,128)(2,1)S(1)}, u32[]{:S(2)}, u32[]{:S(2)}) collective-permute-start(bf16[512,1792]{1,0:T(8,128)(2,1)} %convert_element_type.58), channel_id=1, source_target_pairs={{0,15},{1,0},{2,1},{3,2},{4,3},{5,4},{6,5},{7,6},{8,7},{9,8},{10,9... | collective-permute-start | bytes 5505032 | tf_op jit(solution)/shard_map/ppermute | solution.py:10
  105.0 0.0 copy-start.1
  105.0 1.9 collective-permute-start.6
  107.0 24.4 %collective-permute-done = bf16[512,1792]{1,0:T(8,128)(2,1)} collective-permute-done((bf16[512,1792]{1,0:T(8,128)(2,1)}, bf16[512,1792]{1,0:T(8,128)(2,1)}, u32[]{:S(2)}, u32[]{:S(2)}) %collective-permute-start) | collective-permute-done | bytes 1835040 | tf_op jit(solution)/shard_map/ppermute | solution.py:10
  131.4 3.0 broadcast_select_fusion
  134.4 0.7 collective-permute-start.1
  135.1 6.4 %collective-permute-done.3 = bf16[512,1792]{1,0:T(8,128)(2,1)S(1)} collective-permute-done((bf16[512,1792]{1,0:T(8,128)(2,1)}, bf16[512,1792]{1,0:T(8,128)(2,1)S(1)}, u32[]{:S(2)}, u32[]{:S(2)}) %collective-permute-start.3) | collective-permute-done | bytes 1835040 | tf_op jit(solution)/shard_map/ppermute | solution.py:10
  141.4 0.0 copy-done.1
  141.4 0.0 copy-start.5
  141.4 1.9 fusion.1
  143.4 1.0 collective-permute-start.4
  144.4 56.9 %collective-permute-done.6 = bf16[512,1792]{1,0:T(8,128)(2,1)} collective-permute-done((bf16[512,1792]{1,0:T(8,128)(2,1)}, bf16[512,1792]{1,0:T(8,128)(2,1)}, u32[]{:S(2)}, u32[]{:S(2)}) %collective-permute-start.6) | collective-permute-done | bytes 1835040 | tf_op jit(solution)/shard_map/ppermute | solution.py:16
  201.3 3.3 fusion.2
  204.6 2.1 broadcast.12
  206.7 1.8 dynamic_update_slice.3
  208.5 0.0 copy-start.4
  208.5 0.0 copy-start.6
  208.5 0.0 collective-permute-done.1
  208.5 3.1 broadcast_select_fusion.1
  211.6 0.0 collective-permute-start.2
  211.6 0.0 copy-done.4
  211.7 0.0 copy-done.6
  211.7 0.0 copy-start.2
  211.7 5.4 %select_convert_fusion = (bf16[512,1792]{1,0:T(8,128)(2,1)}, f32[512,1792]{1,0:T(8,128)}) fusion(f32[512,1792]{1,0:T(8,128)S(1)} %copy-done.4, pred[]{:T(512)S(6)} %lt.30, f32[1,112,1792]{2,1,0:T(8,128)S(1)} %copy-done.6, bf16[512,1792]{1,0:T(8,128)(2,1)} %collective-permute-done.6, s32[]{:T(128)S(6)} %select_n.96, ...), kind=kOutput, calls=%fused_computation.2 | convolution fusion | flops 1234100224 | bytes 10241536 | tf_op jit(solution)/shard_map/dot_general | solution.py:64
  217.1 0.0 collective-permute-start.7
  217.1 0.8 collective-permute-done.4
  217.9 0.0 copy-done.5
  217.9 0.0 copy-done.2
  217.9 3.5 fusion.8
  221.4 2.4 collective-permute-start.5
  223.8 70.5 %collective-permute-done.2 = bf16[512,1792]{1,0:T(8,128)(2,1)} collective-permute-done((bf16[512,1792]{1,0:T(8,128)(2,1)}, bf16[512,1792]{1,0:T(8,128)(2,1)}, u32[]{:S(2)}, u32[]{:S(2)}) %collective-permute-start.2) | collective-permute-done | bytes 1835040 | tf_op jit(solution)/shard_map/ppermute | solution.py:10
  294.3 0.0 copy-start.3
  294.3 19.6 %fusion.4 = f32[512,1792]{1,0:T(8,128)} fusion(bf16[512,1792]{1,0:T(8,128)(2,1)} %collective-permute-done.2, bf16[512,1792]{1,0:T(8,128)(2,1)} %broadcast_select_fusion.1, pred[]{:T(512)S(6)} %eq.32, f32[1,1,1792,1792]{3,2,1,0:T(8,128)} %param.9), kind=kOutput, calls=%fused_computation.12 | convolution fusion | flops 19730923520 | bytes 20185088 | tf_op jit(solution)/shard_map/dot_general | solution.py:40
  313.9 0.0 collective-permute-done.7
  313.9 0.0 collective-permute-done.5
  313.9 0.0 copy-done.3
  313.9 8.0 %add_convert_fusion = bf16[512,1792]{1,0:T(8,128)(2,1)} fusion(bf16[512,1792]{1,0:T(8,128)(2,1)} %collective-permute-done.7, f32[512,1792]{1,0:T(8,128)} %dynamic_update_slice.3, f32[512,1792]{1,0:T(8,128)} %get-tuple-element.16, f32[512,1792]{1,0:T(8,128)} %fusion.4, bf16[512,1792]{1,0:T(8,128)(2,1)} %collective-permute-done.5, pred[]{:T(512)S(6)} %lt.30, ...), kind=kLoop, calls=%fused_computation.1 | loop fusion | flops 11010048 | bytes 23855108 | tf_op jit(solution)/shard_map/convert_element_type | solution.py:73
  321.9 0.0 all-gather.3.cloned.1.call-update
  322.0 145.5 %all-gather.3.cloned.1.call-done = bf16[4096,1792]{1,0:T(8,128)(2,1)} async-done(((bf16[512,1792]{1,0:T(8,128)(2,1)}), bf16[4096,1792]{1,0:T(8,128)(2,1)}) %all-gather.3.cloned.1.call-update) | async-done | bytes 14680080 | tf_op jit(solution)/shard_map/all_gather | solution.py:73
  467.5 8.4 %reduce_sum.22 = bf16[512,1792]{1,0:T(8,128)(2,1)S(1)} reduce(bf16[8,512,1792]{2,1,0:T(8,128)(2,1)} %bitcast.18, bf16[]{:T(256)} %constant.70.clone.1), dimensions={0}, to_apply=%region_4.5 | reduce | flops 6422528 | bytes 16515074 | tf_op jit(solution)/shard_map/reduce_sum | solution.py:73
  475.8 0.0 copy-done
  475.8 3.9 fusion
  479.7 5.9 %copy.10 = bf16[1024,1792]{1,0:T(8,128)(2,1)} copy(bf16[1024,1792]{0,1:T(8,128)(2,1)} %fusion) | data formatting | bytes 7340032 | tf_op jit(solution)/shard_map/convert_element_type | solution.py:74
Async XLA Ops:
  6.5 469.3 %copy-start = (bf16[1024,512]{1,0:T(8,128)(2,1)S(1)}, bf16[1024,512]{1,0:T(8,128)(2,1)}, u32[]{:S(2)}) copy-start(bf16[1024,512]{1,0:T(8,128)(2,1)} %param.11) | copy-start | bytes 3145732
  6.5 87.6 %all-reduce.2.cloned.1.call-start = ((), (), s32[]{:S(2)}) async-start(), calls=%async_computation | async-start | bytes 3670016 | tf_op jit(solution)/shard_map/psum | solution.py:32
  10.8 456.7 %all-gather.3.cloned.1.call-start = ((), (), s32[]{:S(2)}) async-start(), calls=%async_computation.1 | async-start | bytes 16515072 | tf_op jit(solution)/shard_map/all_gather | solution.py:73
  94.1 37.3 %collective-permute-start = (bf16[512,1792]{1,0:T(8,128)(2,1)}, bf16[512,1792]{1,0:T(8,128)(2,1)}, u32[]{:S(2)}, u32[]{:S(2)}) collective-permute-start(bf16[512,1792]{1,0:T(8,128)(2,1)} %all-reduce.2.cloned.1.call-done), channel_id=1, source_target_pairs={{0,1},{1,2},{2,3},{3,4},{4,5},{5,6},{6,7},{7,8},{8,9},{9,10},{10,1... | collective-permute-start | bytes 5505032 | tf_op jit(solution)/shard_map/ppermute | solution.py:10
  99.7 41.7 %collective-permute-start.3 = (bf16[512,1792]{1,0:T(8,128)(2,1)}, bf16[512,1792]{1,0:T(8,128)(2,1)S(1)}, u32[]{:S(2)}, u32[]{:S(2)}) collective-permute-start(bf16[512,1792]{1,0:T(8,128)(2,1)} %convert_element_type.58), channel_id=1, source_target_pairs={{0,15},{1,0},{2,1},{3,2},{4,3},{5,4},{6,5},{7,6},{8,7},{9,8},{10,9... | collective-permute-start | bytes 5505032 | tf_op jit(solution)/shard_map/ppermute | solution.py:10
  105.0 36.4 %copy-start.1 = (f32[512,1792]{1,0:T(8,128)S(1)}, f32[512,1792]{1,0:T(8,128)}, u32[]{:S(2)}) copy-start(f32[512,1792]{1,0:T(8,128)} %get-tuple-element.17) | copy-start | bytes 11010052
  105.0 96.3 %collective-permute-start.6 = (bf16[512,1792]{1,0:T(8,128)(2,1)}, bf16[512,1792]{1,0:T(8,128)(2,1)}, u32[]{:S(2)}, u32[]{:S(2)}) collective-permute-start(bf16[512,1792]{1,0:T(8,128)(2,1)} %all-reduce.2.cloned.1.call-done), channel_id=1, source_target_pairs={{0,8},{1,9},{2,10},{3,11},{4,12},{5,13},{6,14},{7,15},{8,0},{9,1},... | collective-permute-start | bytes 5505032 | tf_op jit(solution)/shard_map/ppermute | solution.py:16
  134.4 74.1 %collective-permute-start.1 = (bf16[512,1792]{1,0:T(8,128)(2,1)}, bf16[512,1792]{1,0:T(8,128)(2,1)}, u32[]{:S(2)}, u32[]{:S(2)}) collective-permute-start(bf16[512,1792]{1,0:T(8,128)(2,1)} %broadcast_select_fusion), channel_id=1, source_target_pairs={{0,2},{1,3},{2,4},{3,5},{4,6},{5,7},{6,8},{7,9},{8,10},{9,11},{10,... | collective-permute-start | bytes 5505032 | tf_op jit(solution)/shard_map/ppermute | solution.py:10
  141.4 76.5 %copy-start.5 = (bf16[512,1792]{1,0:T(8,128)(2,1)}, bf16[512,1792]{1,0:T(8,128)(2,1)S(1)}, u32[]{:S(2)}) copy-start(bf16[512,1792]{1,0:T(8,128)(2,1)S(1)} %collective-permute-done.3) | copy-start | bytes 5505028
  143.4 74.5 %collective-permute-start.4 = (bf16[512,1792]{1,0:T(8,128)(2,1)}, bf16[512,1792]{1,0:T(8,128)(2,1)}, u32[]{:S(2)}, u32[]{:S(2)}) collective-permute-start(bf16[512,1792]{1,0:T(8,128)(2,1)} %fusion.1), channel_id=1, source_target_pairs={{0,14},{1,15},{2,0},{3,1},{4,2},{5,3},{6,4},{7,5},{8,6},{9,7},{10,... | collective-permute-start | bytes 5505032 | tf_op jit(solution)/shard_map/ppermute | solution.py:10
  208.5 3.2 copy-start.4
  208.5 3.2 copy-start.6
  211.6 82.7 %collective-permute-start.2 = (bf16[512,1792]{1,0:T(8,128)(2,1)}, bf16[512,1792]{1,0:T(8,128)(2,1)}, u32[]{:S(2)}, u32[]{:S(2)}) collective-permute-start(bf16[512,1792]{1,0:T(8,128)(2,1)} %broadcast_select_fusion.1), channel_id=1, source_target_pairs={{0,4},{1,5},{2,6},{3,7},{4,8},{5,9},{6,10},{7,11},{8,12},{9,13},{1... | collective-permute-start | bytes 5505032 | tf_op jit(solution)/shard_map/ppermute | solution.py:10
  211.7 6.3 %copy-start.2 = (f32[512,1792]{1,0:T(8,128)S(1)}, f32[512,1792]{1,0:T(8,128)}, u32[]{:S(2)}) copy-start(f32[512,1792]{1,0:T(8,128)} %get-tuple-element.17) | copy-start | bytes 11010052
  217.1 96.8 %collective-permute-start.7 = (bf16[512,1792]{1,0:T(8,128)(2,1)}, bf16[512,1792]{1,0:T(8,128)(2,1)}, u32[]{:S(2)}, u32[]{:S(2)}) collective-permute-start(bf16[512,1792]{1,0:T(8,128)(2,1)} %get-tuple-element.15), channel_id=1, source_target_pairs={{0,8},{1,9},{2,10},{3,11},{4,12},{5,13},{6,14},{7,15},{8,0},{9,1},... | collective-permute-start | bytes 5505032 | tf_op jit(solution)/shard_map/ppermute | solution.py:16
  221.4 92.5 %collective-permute-start.5 = (bf16[512,1792]{1,0:T(8,128)(2,1)}, bf16[512,1792]{1,0:T(8,128)(2,1)}, u32[]{:S(2)}, u32[]{:S(2)}) collective-permute-start(bf16[512,1792]{1,0:T(8,128)(2,1)} %fusion.8), channel_id=1, source_target_pairs={{0,12},{1,13},{2,14},{3,15},{4,0},{5,1},{6,2},{7,3},{8,4},{9,5},{1... | collective-permute-start | bytes 5505032 | tf_op jit(solution)/shard_map/ppermute | solution.py:10
  294.3 19.6 %copy-start.3 = (f32[512,1792]{1,0:T(8,128)S(1)}, f32[512,1792]{1,0:T(8,128)}, u32[]{:S(2)}) copy-start(f32[512,1792]{1,0:T(8,128)} %get-tuple-element.17) | copy-start | bytes 11010052
Sparse Core Ops, SparseCore 0:
  10.9 83.1 all-reduce.1
  322.1 145.3 all-gather.2
